TPU v7x, 768 devices: a whole 4x8x12 slice. The times are simulated.
768 devices in a mesh: rep: 12 (over z_hi, x), shard: 64 (over y, z_lo, core).
Axes of the slice: x: 4, y: 8, z: 12 (z_hi: 3, z_lo: 4; z = z_hi * 4 + z_lo), core: 2. Of those that a mesh axis runs over, the one named last changes fastest.
Arguments:
- activations: bfloat16 [1536, 12288], P('rep', 'shard'), may hold values from -6 to 6
- cotangent: bfloat16 [1536, 8192], P('rep', 'shard'), may hold values from -0.15625 to 0.15625
- weight: bfloat16 [12288, 8192], P('shard'), may hold values from -2.5 to 2.5
- master: float32 [12288, 8192], P(('shard', 'rep')), may hold values from -0.12 to 0.12
- moment: float32 [12288, 8192], P(('shard', 'rep')), may hold values from -1.2 to 1.2
- second: float32 [12288, 8192], P(('shard', 'rep')), may hold values from 0.1 to 2
- average: float32 [12288, 8192], P(('shard', 'rep')), may hold values from -0.12 to 0.12
Outputs:
- new_master: float32 [12288, 8192], P(('shard', 'rep'))
- new_moment: float32 [12288, 8192], P(('shard', 'rep'))
- new_second: float32 [12288, 8192], P(('shard', 'rep'))
- new_average: float32 [12288, 8192], P(('shard', 'rep'))
- parameters: bfloat16 [12288, 8192], P('shard')
- grad_hidden: bfloat16 [1536, 12288], P('rep', 'shard')
All inputs are finite; a program needn't handle non-finite values.
Results may differ from a plain program's by a relative error of at most 0.0065.
Values may be sent and summed in bfloat16 or wider, within the bound.
A program may use at most 64 MiB of HBM per device.

v0:
```python
import jax
import jax.numpy as jnp
from jax import lax
from jax.sharding import PartitionSpec as P

STEP = 10


def shards(activations, cotangent, weight, master, moment, second, average):
    features = lax.all_gather(cotangent, "shard", axis=1, tiled=True)
    hidden_grad = lax.dot_general(
        features, weight, (((1,), (1,)), ((), ())), preferred_element_type=jnp.float32
    )
    weight_grad = lax.dot_general(
        activations, features, (((0,), (0,)), ((), ())), preferred_element_type=jnp.float32
    )
    gradient = lax.psum_scatter(
        weight_grad.astype(jnp.bfloat16), "rep", scatter_dimension=0, tiled=True
    ).astype(jnp.float32)
    first_fix = 1.0 - 0.9**STEP
    second_fix = 1.0 - 0.999**STEP
    ema_decay = min(0.999, (1.0 + STEP) / (10.0 + STEP))
    new_moment = 0.9 * moment + 0.1 * gradient
    new_second = 0.999 * second + 0.001 * gradient * gradient
    update = new_moment / first_fix / (jnp.sqrt(new_second / second_fix) + 1e-08) + 0.1 * master
    new_master = master - 0.01 * update
    new_average = ema_decay * average + (1.0 - ema_decay) * new_master
    parameters = lax.all_gather(new_master.astype(jnp.bfloat16), "rep", axis=0, tiled=True)
    return (
        new_master,
        new_moment,
        new_second,
        new_average,
        parameters,
        hidden_grad.astype(jnp.bfloat16),
    )


def solution(mesh):
    in_specs = (
        P("rep", "shard"),
        P("rep", "shard"),
        P("shard", None),
        P(("shard", "rep"), None),
        P(("shard", "rep"), None),
        P(("shard", "rep"), None),
        P(("shard", "rep"), None),
    )
    out_specs = (
        P(("shard", "rep"), None),
        P(("shard", "rep"), None),
        P(("shard", "rep"), None),
        P(("shard", "rep"), None),
        P("shard", None),
        P("rep", "shard"),
    )
    return jax.shard_map(shards, mesh=mesh, in_specs=in_specs, out_specs=out_specs, check_vma=False)
```

profile of v0, /device:TPU:192, one launch (start us, length us, event | category | flops | bytes accessed | tf_op | source)
XLA Modules:
  0.0 452.9 jit_solution(10082172992667577602)
XLA Ops:
  7.2 0.0 copy-start
  7.2 0.0 all-gather.3.cloned.1.call-start
  7.2 0.7 all-gather.3.cloned.1.call-update
  7.9 0.0 reduce-scatter.2.cloned.1.call-start
  8.0 124.5 %all-gather.3.cloned.1.call-done = bf16[128,8192]{1,0:T(8,128)(2,1)} async-done(((bf16[128,128]{1,0:T(8,128)(2,1)}), bf16[128,8192]{1,0:T(8,128)(2,1)}) %all-gather.3.cloned.1.call-update) | async-done | bytes 2097168 | tf_op jit(solution)/shard_map/all_gather | solution.py:10
  132.5 4.3 convolution_convert_fusion
  136.7 0.0 reduce-scatter.2.cloned.1.call-update
  136.8 0.0 all-gather.5.cloned.1.call-start
  136.8 191.6 %reduce-scatter.2.cloned.1.call-done = bf16[16,8192]{1,0:T(8,128)(2,1)} async-done(((bf16[192,8192]{1,0:T(8,128)(2,1)}), bf16[16,8192]{1,0:T(8,128)(2,1)}) %reduce-scatter.2.cloned.1.call-update) | async-done | bytes 262160 | tf_op jit(solution)/shard_map/reduce_scatter | solution.py:17
  328.4 2.9 fusion.2
  331.3 0.0 all-gather.5.cloned.1.call-update
  331.3 0.0 copy-done
  331.3 0.0 copy-start.1
  331.3 0.0 copy-start.2
  331.3 3.3 convolution_convert_fusion.1
  334.6 0.0 copy-done.1
  334.6 0.0 copy-done.2
  334.6 0.9 multiply_add_fusion
  335.5 107.0 %all-gather.5.cloned.1.call-done = bf16[192,8192]{1,0:T(8,128)(2,1)} async-done(((bf16[16,8192]{1,0:T(8,128)(2,1)}), bf16[192,8192]{1,0:T(8,128)(2,1)}) %all-gather.5.cloned.1.call-update) | async-done | bytes 3145744 | tf_op jit(solution)/shard_map/all_gather | solution.py:28
  442.5 3.9 copy.14
Async XLA Ops:
  7.2 324.2 %copy-start = (bf16[192,8192]{1,0:T(8,128)(2,1)S(1)}, bf16[192,8192]{1,0:T(8,128)(2,1)}, u32[]{:S(2)}) copy-start(bf16[192,8192]{1,0:T(8,128)(2,1)} %param.9) | copy-start | bytes 9437188
  7.2 125.3 %all-gather.3.cloned.1.call-start = ((), (), s32[]{:S(2)}) async-start(), calls=%async_computation.1 | async-start | bytes 2129920 | tf_op jit(solution)/shard_map/all_gather | solution.py:10
  7.9 320.5 %reduce-scatter.2.cloned.1.call-start = ((), (), s32[]{:S(2)}) async-start(), calls=%async_computation.2 | async-start | bytes 3407872 | tf_op jit(solution)/shard_map/reduce_scatter | solution.py:17
  136.8 305.8 %all-gather.5.cloned.1.call-start = ((), (), s32[]{:S(2)}) async-start(), calls=%async_computation.3 | async-start | bytes 3407872 | tf_op jit(solution)/shard_map/all_gather | solution.py:28
  331.3 3.3 copy-start.1
  331.3 3.3 copy-start.2
Sparse Core Ops, SparseCore 0:
  10.4 122.0 all-gather.2
  138.5 189.8 reduce-scatter.1
  333.6 108.8 all-gather.4
where the time goes:
time: 453 us
  waiting for transfers between devices  424 us (94%)
  between operations  13.8 us (3%)
  matrix products  7.52 us (2%)
    reduce_scatter x1, waiting for transfers between devices, shards(): lax.psum_scatter(weight_grad.astype(jnp.bfloat16), 'rep', scatter_dimensi...  192 us
    all_gather x1, waiting for transfers between devices, shards(): features = lax.all_gather(cotangent, 'shard', axis=1, tiled=True)  125 us
    all_gather x1, waiting for transfers between devices, shards(): lax.all_gather(new_master.astype(jnp.bfloat16), 'rep', axis=0, tiled=True)  107 us
  transfers between devices with their start and end apart: 3, of which 3 were waited for; matrix products, arithmetic and copies ran while one was open for 1% of the time, Pallas kernels for 0%

commit v1 on v0

v1 whole, which is shorter than its diff:
```python
import jax
import jax.numpy as jnp
from jax import lax
from jax.experimental import pallas as pl
from jax.experimental.pallas import tpu as pltpu
from jax.sharding import PartitionSpec as P

STEP = 10
MESH = pl.DeviceIdType.MESH
F32, BF16 = jnp.float32, jnp.bfloat16
NX, NY, NZ, NH, NL = 4, 8, 12, 3, 4
TOK, FB = 128, 128
K = NH * TOK
UNITS, UC = 16, 512
YT = 14
LAG_C, LAG_D, LAG_E, LAG_G = 2, 4, 6, 8


def chip(x, y, z, c):
    return ((z // NL) * NX + x, (y * NL + z % NL) * 2 + c)


def unit_place(u):
    j = jnp.maximum(u - 2, 0)
    s = j // 4 + 1
    slot = jnp.where(u < 2, 0, jnp.where(j % 2 == 0, s, NY - s))
    pair = jnp.where(u < 2, u, jnp.where(u == UNITS - 1, 1, (j // 2) % 2))
    return slot, pair


def kernel(
    act_t, cot, weight, master, moment, second, average,
    o_master, o_moment, o_second, o_average, o_params, o_hidden,
    feats, at_v, lhs_all, lhs, wv, st, part, got, own, par, acc,
    in_sem, a_s, a_r, f_s, f_r, b_s, b_r, yp_s, yp_r, ym_s, ym_r, c_s, c_r,
    r_s, r_r, z_s, z_r, x_s, x_r, w_s, w_r,
):
    rep, shard = lax.axis_index("rep"), lax.axis_index("shard")
    zh, x = rep // NX, rep % NX
    y, zl, c = shard // 8, (shard // 2) % NL, shard % 2
    z = zh * NL + zl

    def at(dx=0, dy=0, dz=0):
        return chip((x + dx) % NX, (y + dy) % NY, (z + dz) % NZ, c)

    partner = chip(x, y, z, 1 - c)
    far = 2 + 8 * c
    far_back = 10 - 8 * c
    turn = 1 + 2 * c

    def send(src, dst, ssem, rsem, to):
        return pltpu.make_async_remote_copy(
            src_ref=src, dst_ref=dst, send_sem=ssem, recv_sem=rsem, device_id=to, device_id_type=MESH
        )

    loads = [
        pltpu.make_async_copy(cot, feats.at[0, c, 0, pl.ds(zh * TOK, TOK)], in_sem.at[0]),
        pltpu.make_async_copy(act_t, at_v, in_sem.at[1]),
        pltpu.make_async_copy(weight, wv, in_sem.at[2]),
    ] + [
        pltpu.make_async_copy(ref, st.at[n], in_sem.at[3 + n])
        for n, ref in enumerate((master, moment, second, average))
    ]
    for load in loads:
        load.start()

    barrier = pltpu.get_barrier_semaphore()
    sources = [at(dz=4), at(dz=8), at(dz=1), at(dz=11), at(dz=far_back), at(dy=1), at(dy=7), at(dx=1), at(dx=2), at(dx=3), partner]
    for source in sources:
        pl.semaphore_signal(barrier, inc=1, device_id=source, device_id_type=MESH)
    pl.semaphore_wait(barrier, len(sources))

    loads[0].wait()
    mine = feats.at[0, c, 0, pl.ds(zh * TOK, TOK)]
    for d in (1, 2):
        send(mine, mine, f_s.at[d - 1], f_r.at[d - 1], at(dz=4 * d)).start()
    loads[1].wait()
    lhs_all[zh] = at_v[pl.ds(pl.multiple_of(zh * 64, 64), 64), :]

    def act_copy(d):
        rows = pl.ds(pl.multiple_of(((zh + d) % NH) * 64, 64), 64)
        return send(at_v.at[rows], lhs_all.at[zh], a_s.at[d - 1], a_r.at[d - 1], at(dz=4 * d))

    for d in (1, 2):
        act_copy(d).start()
    for d in (1, 2):
        send(mine, mine, f_s.at[d - 1], f_r.at[d - 1], at(dz=4 * d)).wait_recv()

    first = feats.at[0, c, 0]

    def bundle(n):
        to = (1, 11, far)[n]
        return send(first, feats.at[0, c, (2, 1, 3)[n]], b_s.at[n], b_r.at[n], at(dz=to))

    for n in range(3):
        bundle(n).start()

    def y_plus(s, i, j):
        return send(feats.at[s, c, i], feats.at[s + 1, c, i], yp_s.at[j], yp_r.at[j], at(dy=1))

    def y_minus(s, i, j):
        return send(
            feats.at[(NY - s) % NY, c, i], feats.at[NY - s - 1, c, i], ym_s.at[j], ym_r.at[j], at(dy=7)
        )

    def across(u):
        slot, pair = unit_place(u)
        ref = feats.at[slot, c, pl.ds(pair * 2, 2)]
        return send(ref, ref, c_s.at[u], c_r.at[u], partner)

    for i in range(4):
        if i:
            bundle((1, 0, 2)[i - 1]).wait_recv()
        y_plus(0, i, i).start()
        y_minus(0, i, i).start()
        if i % 2:
            across(i // 2).start()

    for d in (1, 2):
        act_copy(d).wait_recv()
    for d in range(NX):
        rows = pl.ds(pl.multiple_of(((x + d) % NX) * 16, 16), 16)
        for h in range(NH):
            lhs[d * 16 : (d + 1) * 16, h * TOK : (h + 1) * TOK] = lhs_all[h, rows, :]
    acc[...] = jnp.zeros_like(acc)
    for load in loads[2:]:
        load.wait()

    def columns(u, k):
        slot, pair = unit_place(u)
        i = pair * 2 + k
        low = (zl + jnp.where(i == 2, 3, jnp.where(i == 3, 2, i))) % NL
        return pl.ds(pl.multiple_of(((y - slot + NY) % NY) * 1024 + low * 256, 256), 256)

    def reduce_copy(u, d):
        return send(part.at[u, d - 1], got.at[u, d - 1], r_s.at[u, d - 1], r_r.at[u, d - 1], at(dx=d))

    def z_copy(u, d):
        return send(par.at[u, 0, 0], par.at[u, 0, NH - d], z_s.at[u, d - 1], z_r.at[u, d - 1], at(dz=4 * d))

    def x_copy(u, n):
        return send(par.at[u, 0], par.at[u, 3 - 2 * n], x_s.at[u, n], x_r.at[u, n], at(dx=1 + 2 * n))

    def w_copy(u):
        return send(par.at[u, 3 - 2 * c], par.at[u, 2], w_s.at[u], w_r.at[u], at(dx=turn))

    first_fix = 1.0 - 0.9**STEP
    second_fix = 1.0 - 0.999**STEP
    decay = min(0.999, (1.0 + STEP) / (10.0 + STEP))

    def pass_on(j):
        s, i = j // 4 + 1, j % 4
        i_minus = i + jnp.where(j >= 12, 2, 0)
        y_plus(s - 1, i, j).wait_recv()

        @pl.when(j < 10)
        def _():
            y_plus(s, i, j + 4).start()

        y_minus(s - 1, i_minus, j).wait_recv()

        @pl.when((j < 8) | ((j >= 10) & (j < 12)))
        def _():
            y_minus(s, i_minus, jnp.where(j < 8, j + 4, j + 2)).start()

        @pl.when(j % 2 == 1)
        def _():
            across(j + 1).start()
            across(j + 2).start()

    def multiply(u):
        slot, pair = unit_place(u)
        across(u).wait_recv()
        for k in (0, 1):
            i = pair * 2 + k
            right = jnp.concatenate([feats[slot, 0, i], feats[slot, 1, i]], axis=1)
            grad = jnp.dot(lhs[...], right, preferred_element_type=F32)
            own[u, :, k * 256 : (k + 1) * 256] = grad[:16]
            for d in range(1, NX):
                part[u, d - 1, :, k * 256 : (k + 1) * 256] = grad[d * 16 : (d + 1) * 16].astype(BF16)
        for d in (2, 1, 3):
            reduce_copy(u, d).start()
        for k in (0, 1):
            i = pair * 2 + k
            rows = pl.ds(pl.multiple_of(zh * TOK, TOK), TOK)
            left = jnp.concatenate([feats[slot, 0, i, rows, :], feats[slot, 1, i, rows, :]], axis=1)
            acc[...] += lax.dot_general(
                wv[:, columns(u, k)], left, (((1,), (1,)), ((), ())), preferred_element_type=F32
            )

    def update(u):
        for d in (1, 2, 3):
            reduce_copy(u, d).wait_recv()
        for k in (0, 1):
            here, cols = slice(k * 256, (k + 1) * 256), columns(u, k)
            gradient = own[u, :, here]
            for d in (1, 2, 3):
                gradient = gradient + got[u, d - 1, :, here].astype(F32)
            new_moment = 0.9 * st[1, :, cols] + 0.1 * gradient
            new_second = 0.999 * st[2, :, cols] + 0.001 * gradient * gradient
            old = st[0, :, cols]
            step = new_moment / first_fix / (jnp.sqrt(new_second / second_fix) + 1e-08) + 0.1 * old
            new_master = old - 0.01 * step
            par[u, 0, 0, :, here] = new_master.astype(BF16)
            o_master[:, cols] = new_master
            o_moment[:, cols] = new_moment
            o_second[:, cols] = new_second
            o_average[:, cols] = decay * st[3, :, cols] + (1.0 - decay) * new_master
        for d in (1, 2):
            z_copy(u, d).start()

    def spread_x(u):
        for d in (1, 2):
            z_copy(u, d).wait_recv()
        for n in (0, 1):
            x_copy(u, n).start()

    def spread_far(u):
        x_copy(u, c).wait_recv()
        w_copy(u).start()

    def finish(u):
        x_copy(u, 1 - c).wait_recv()
        w_copy(u).wait_recv()
        for a in range(NX):
            for b in range(NH):
                rows = pl.ds(pl.multiple_of((((zh + b) % NH) * NX + (x + a) % NX) * 16, 16), 16)
                for k in (0, 1):
                    o_params[rows, columns(u, k)] = par[u, a, b, :, k * 256 : (k + 1) * 256]
        across(u).wait_send()
        for d in (1, 2, 3):
            reduce_copy(u, d).wait_send()
        for d in (1, 2):
            z_copy(u, d).wait_send()
        for n in (0, 1):
            x_copy(u, n).wait_send()
        w_copy(u).wait_send()

        @pl.when(u < YT)
        def _():
            y_plus(0, 0, u).wait_send()
            y_minus(0, 0, u).wait_send()

    def tick(t, _):
        def stage(f, lag, count=UNITS):
            u = t - lag

            @pl.when((u >= 0) & (u < count))
            def _():
                f(u)

        stage(pass_on, 0, YT)
        stage(spread_far, LAG_E)
        stage(spread_x, LAG_D)
        stage(update, LAG_C)
        stage(multiply, 0)
        stage(finish, LAG_G)
        return 0

    lax.fori_loop(0, UNITS + LAG_G, tick, 0)
    o_hidden[...] = acc[...].astype(BF16)
    for d in (1, 2):
        send(mine, mine, f_s.at[d - 1], f_r.at[d - 1], at(dz=4 * d)).wait_send()
        act_copy(d).wait_send()
    for n in range(3):
        bundle(n).wait_send()


def shards(activations, cotangent, weight, master, moment, second, average):
    rows, width = master.shape
    hidden = weight.shape[0]
    dma = pltpu.SemaphoreType.DMA
    vmem = pltpu.VMEM
    operands = (activations.T, cotangent, weight, master, moment, second, average)
    operands = [pltpu.with_memory_space_constraint(a, pltpu.HBM) for a in operands]
    *updated, hidden_grad = pl.pallas_call(
        kernel,
        out_shape=[vmem((rows, width), F32)] * 4 + [vmem((hidden, width), BF16), vmem((hidden, TOK), BF16)],
        in_specs=[pl.BlockSpec(memory_space=pltpu.HBM)] * 7,
        out_specs=[pl.BlockSpec(memory_space=pltpu.VMEM)] * 6,
        scratch_shapes=[
            vmem((NY, 2, NL, K, FB), BF16),
            vmem((hidden, TOK), BF16),
            vmem((NH, hidden // NH, TOK), BF16),
            vmem((hidden // NH, K), BF16),
            vmem((hidden, width), BF16),
            vmem((4, rows, width), F32),
            vmem((UNITS, 3, 16, UC), BF16),
            vmem((UNITS, 3, 16, UC), BF16),
            vmem((UNITS, 16, UC), F32),
            vmem((UNITS, NX, NH, 16, UC), BF16),
            vmem((hidden, TOK), F32),
            dma((7,)),
            dma((2,)), dma((2,)), dma((2,)), dma((2,)), dma((3,)), dma((3,)),
            dma((YT,)), dma((YT,)), dma((YT,)), dma((YT,)), dma((UNITS,)), dma((UNITS,)),
            dma((UNITS, 3)), dma((UNITS, 3)), dma((UNITS, 2)), dma((UNITS, 2)),
            dma((UNITS, 2)), dma((UNITS, 2)), dma((UNITS,)), dma((UNITS,)),
        ],
        compiler_params=pltpu.CompilerParams(
            collective_id=0, has_side_effects=True, vmem_limit_bytes=22 * 1024 * 1024
        ),
    )(*operands)
    return *updated, hidden_grad.T


def solution(mesh):
    row = P(("shard", "rep"), None)
    both = P("rep", "shard")
    wide = P("shard", None)
    return jax.shard_map(
        shards,
        mesh=mesh,
        in_specs=(both, both, wide, row, row, row, row),
        out_specs=(row, row, row, row, wide, both),
        check_vma=False,
    )
```

time: 453 us -> 95 us (0.21)
  the two profiles are of different devices: /device:TPU:192 before, /device:TPU:24 now
where the time goes in v1:
time: 95 us; the launch traced here: 94.9 us
  Pallas kernels  88.8 us (93%)
  local copies, waits for them, and re-layouts  5.46 us (6%)
    pallas_call x1, Pallas kernels, shards(): pl.pallas_call(kernel, out_shape=[vmem((rows, width), F32)] * 4 + [vmem((...  88.8 us
    unnamed x6, local copies, waits for them, and re-layouts  5.46 us

profile of v1, /device:TPU:24, one launch (start us, length us, event | category | flops | bytes accessed | tf_op | source)
XLA Modules:
  0.0 94.9 jit_solution(1541859135614017671)
XLA Ops:
  0.6 88.8 %shard_map.118 = (f32[16,8192]{1,0:T(8,128)S(1)}, f32[16,8192]{1,0:T(8,128)S(1)}, f32[16,8192]{1,0:T(8,128)S(1)}, f32[16,8192]{1,0:T(8,128)S(1)}, bf16[192,8192]...) custom-call(bf16[192,128]{1,0:T(8,128)(2,1)} %bitcast.3, bf16[128,128]{1,0:T(8,128)(2,1)} %cot.1, bf16[192,8192]{1,0:T(8,128)(2,1)} %weight.1, ...), custom_call_target="tpu_custom_call" | custom-call | tf_op jit(solution)/shard_map/pallas_call | solution.py:276
  89.4 0.8 copy.19
  90.2 0.6 copy.24
  90.8 0.8 copy.20
  91.6 0.8 copy.21
  92.4 0.8 copy.22
  93.2 1.7 %copy.23 = bf16[192,8192]{1,0:T(8,128)(2,1)} copy(bf16[192,8192]{1,0:T(8,128)(2,1)S(1)} %get-tuple-element.22) | data formatting | bytes 6291456

commit v2 on v1

v2 whole, which is shorter than its diff:
```python
import jax
import jax.numpy as jnp
from jax import lax
from jax.experimental import pallas as pl
from jax.experimental.pallas import tpu as pltpu
from jax.sharding import PartitionSpec as P

STEP = 10
MESH = pl.DeviceIdType.MESH
F32, BF16 = jnp.float32, jnp.bfloat16
NX, NY, NZ, NH, NL = 4, 8, 12, 3, 4
TOK, FB = 128, 128
K = NH * TOK
UNITS, UC = 16, 512
YT = 14
LAG_C, LAG_D, LAG_E, LAG_G = 2, 5, 8, 10
LAG_H = 4


def chip(x, y, z, c):
    return ((z // NL) * NX + x, (y * NL + z % NL) * 2 + c)


ORDER = (
    (0, 0), (0, 1), (1, 0), (7, 0), (1, 1), (7, 1), (2, 0), (6, 0),
    (2, 1), (6, 1), (3, 0), (5, 0), (3, 1), (5, 1), (4, 0), (4, 1),
)
STEPS = (
    (0, 2, 4, 4, 6, 6, 8, 8, 10, 10, 12, 12, 14, 14, 14, 14),
    (0, 0, 0, 2, 4, 4, 6, 6, 8, 8, 10, 10, 12, 12, 14, 14),
)


def pick(table, n):
    value = table[0]
    for k in range(1, len(table)):
        if table[k] != table[k - 1]:
            value = jnp.where(n >= k, table[k], value)
    return value


def unit_place(n):
    return pick([slot for slot, _ in ORDER], n), pick([core for _, core in ORDER], n)


def kernel(
    act_t, cot, weight, master, moment, second, average,
    o_master, o_moment, o_second, o_average, o_params, o_hidden,
    feats, at_v, lhs_all, lhs, wv, st, part, got, own, par, acc,
    in_sem, a_s, a_r, f_s, f_r, b_s, b_r, yp_s, yp_r, ym_s, ym_r, c_s, c_r,
    r_s, r_r, z_s, z_r, x_s, x_r, w_s, w_r, there,
):
    rep, shard = lax.axis_index("rep"), lax.axis_index("shard")
    zh, x = rep // NX, rep % NX
    y, zl, c = shard // 8, (shard // 2) % NL, shard % 2
    z = zh * NL + zl

    def at(dx=0, dy=0, dz=0):
        return chip((x + dx) % NX, (y + dy) % NY, (z + dz) % NZ, c)

    partner = chip(x, y, z, 1 - c)
    far, far_back = at(dz=2 + 8 * c), at(dz=10 - 8 * c)
    turn = at(dx=1 + 2 * c)
    x_at = [None] + [at(dx=n) for n in (1, 2, 3)]
    y_up, y_down = at(dy=1), at(dy=7)
    z_at = [None, at(dz=4), at(dz=8)]
    z_up, z_down = at(dz=1), at(dz=11)

    def send(src, dst, ssem, rsem, to):
        return pltpu.make_async_remote_copy(
            src_ref=src, dst_ref=dst, send_sem=ssem, recv_sem=rsem, device_id=to, device_id_type=MESH
        )

    loads = [
        pltpu.make_async_copy(cot, feats.at[0, c, 0, pl.ds(zh * TOK, TOK)], in_sem.at[0]),
        pltpu.make_async_copy(act_t, at_v, in_sem.at[1]),
        pltpu.make_async_copy(weight, wv, in_sem.at[2]),
    ] + [
        pltpu.make_async_copy(ref, st.at[n], in_sem.at[3 + n])
        for n, ref in enumerate((master, moment, second, average))
    ]
    for load in loads:
        load.start()

    barrier = pltpu.get_barrier_semaphore()
    sources = [*z_at[1:], z_up, z_down, far_back, y_up, y_down, *x_at[1:]]
    for source in sources:
        pl.semaphore_signal(barrier, inc=1, device_id=source, device_id_type=MESH)

    @pl.when(c == 0)
    def _():
        pl.semaphore_signal(barrier, inc=1, device_id=partner, device_id_type=MESH)

    pl.semaphore_wait(barrier, len(sources) + c)

    @pl.when(c == 1)
    def _():
        pl.semaphore_signal(there, inc=1, device_id=partner, device_id_type=MESH)

    loads[0].wait()
    mine = feats.at[0, c, 0, pl.ds(zh * TOK, TOK)]
    for d in (1, 2):
        send(mine, mine, f_s.at[d - 1], f_r.at[d - 1], z_at[d]).start()
    loads[1].wait()
    lhs_all[zh] = at_v[pl.ds(pl.multiple_of(zh * 64, 64), 64), :]

    def act_copy(d):
        rows = pl.ds(pl.multiple_of(((zh + d) % NH) * 64, 64), 64)
        return send(at_v.at[rows], lhs_all.at[zh], a_s.at[d - 1], a_r.at[d - 1], z_at[d])

    for d in (1, 2):
        act_copy(d).start()
    for d in (1, 2):
        send(mine, mine, f_s.at[d - 1], f_r.at[d - 1], z_at[d]).wait_recv()

    first = feats.at[0, c, 0]

    def bundle(n):
        return send(first, feats.at[0, c, (2, 1, 3)[n]], b_s.at[n], b_r.at[n], (z_up, z_down, far)[n])

    for n in range(3):
        bundle(n).start()

    def y_plus(s, i, j):
        return send(feats.at[s, c, i], feats.at[s + 1, c, i], yp_s.at[j], yp_r.at[j], y_up)

    def y_minus(s, i, j):
        return send(
            feats.at[(NY - s) % NY, c, i], feats.at[NY - s - 1, c, i], ym_s.at[j], ym_r.at[j], y_down
        )

    def across(slot):
        ref = feats.at[slot, c]
        return send(ref, ref, c_s.at[slot], c_r.at[slot], partner)

    def across_here(slot):
        ref = feats.at[slot, 1 - c]
        return send(ref, ref, c_s.at[slot], c_r.at[slot], partner)

    for i in range(4):
        if i:
            bundle((1, 0, 2)[i - 1]).wait_recv()
        y_plus(0, i, i).start()
        y_minus(0, i, i).start()

    @pl.when(c == 0)
    def _():
        pl.semaphore_wait(there, 1)

    across(0).start()

    for d in (1, 2):
        act_copy(d).wait_recv()
    for d in range(NX):
        rows = pl.ds(pl.multiple_of(((x + d) % NX) * 16, 16), 16)
        for h in range(NH):
            lhs[d * 16 : (d + 1) * 16, h * TOK : (h + 1) * TOK] = lhs_all[h, rows, :]
    acc[...] = jnp.zeros_like(acc)
    for load in loads[2:]:
        load.wait()

    def columns(u):
        slot, core = unit_place(u)
        low = ((y - slot + NY) % NY) * 1024 + core * 128
        return [pl.ds(pl.multiple_of(low + ((zl + r) % NL) * 256, 128), 128) for r in (0, 1, 3, 2)]

    def reduce_copy(u, d):
        return send(part.at[u, d - 1], got.at[u, d - 1], r_s.at[u, d - 1], r_r.at[u, d - 1], x_at[d])

    def z_copy(u, d):
        return send(par.at[u, 0, 0], par.at[u, 0, NH - d], z_s.at[u, d - 1], z_r.at[u, d - 1], z_at[d])

    def x_copy(u, n):
        return send(par.at[u, 0], par.at[u, 3 - 2 * n], x_s.at[u, n], x_r.at[u, n], x_at[1 + 2 * n] if isinstance(n, int) else turn)

    def w_copy(u):
        return send(par.at[u, 3 - 2 * c], par.at[u, 2], w_s.at[u], w_r.at[u], turn)

    first_fix = 1.0 - 0.9**STEP
    second_fix = 1.0 - 0.999**STEP
    decay = min(0.999, (1.0 + STEP) / (10.0 + STEP))

    def pass_on(j):
        s, i = j // 4 + 1, j % 4
        i_minus = i + jnp.where(j >= 12, 2, 0)
        y_plus(s - 1, i, j).wait_recv()

        @pl.when(j < 10)
        def _():
            y_plus(s, i, j + 4).start()

        y_minus(s - 1, i_minus, j).wait_recv()

        @pl.when((j < 8) | ((j >= 10) & (j < 12)))
        def _():
            y_minus(s, i_minus, jnp.where(j < 8, j + 4, j + 2)).start()

        @pl.when((j % 4 == 3) & (j < 12))
        def _():
            across(s).start()
            across(NY - s).start()

        @pl.when(j == YT - 1)
        def _():
            across(NY // 2).start()

    def multiply(u):
        slot, core = unit_place(u)

        @pl.when(core != c)
        def _():
            across_here(slot).wait_recv()

        for k in (0, 1):
            right = jnp.concatenate([feats[slot, core, 2 * k], feats[slot, core, 2 * k + 1]], axis=1)
            grad = jnp.dot(lhs[...], right, preferred_element_type=F32)
            own[u, :, k * 256 : (k + 1) * 256] = grad[:16]
            for d in range(1, NX):
                part[u, d - 1, :, k * 256 : (k + 1) * 256] = grad[d * 16 : (d + 1) * 16].astype(BF16)
        for d in (2, 1, 3):
            reduce_copy(u, d).start()

    def multiply_hidden(u):
        slot, core = unit_place(u)
        rows = pl.ds(pl.multiple_of(zh * TOK, TOK), TOK)
        left = jnp.concatenate([feats[slot, core, i, rows, :] for i in range(4)], axis=1)
        right = jnp.concatenate([wv[:, run] for run in columns(u)], axis=1)
        acc[...] += lax.dot_general(right, left, (((1,), (1,)), ((), ())), preferred_element_type=F32)

    def update(u):
        for d in (1, 2, 3):
            reduce_copy(u, d).wait_recv()
        for i, cols in enumerate(columns(u)):
            here = slice(i * 128, (i + 1) * 128)
            gradient = own[u, :, here]
            for d in (1, 2, 3):
                gradient = gradient + got[u, d - 1, :, here].astype(F32)
            new_moment = 0.9 * st[1, :, cols] + 0.1 * gradient
            new_second = 0.999 * st[2, :, cols] + 0.001 * gradient * gradient
            old = st[0, :, cols]
            step = new_moment / first_fix / (jnp.sqrt(new_second / second_fix) + 1e-08) + 0.1 * old
            new_master = old - 0.01 * step
            par[u, 0, 0, :, here] = new_master.astype(BF16)
            o_master[:, cols] = new_master
            o_moment[:, cols] = new_moment
            o_second[:, cols] = new_second
            o_average[:, cols] = decay * st[3, :, cols] + (1.0 - decay) * new_master
        for d in (1, 2):
            z_copy(u, d).start()

    def spread_x(u):
        for d in (1, 2):
            z_copy(u, d).wait_recv()
        for n in (0, 1):
            x_copy(u, n).start()

    def spread_far(u):
        x_copy(u, c).wait_recv()
        w_copy(u).start()

    def finish(u):
        x_copy(u, 1 - c).wait_recv()
        w_copy(u).wait_recv()
        for a in range(NX):
            for b in range(NH):
                rows = pl.ds(pl.multiple_of((((zh + b) % NH) * NX + (x + a) % NX) * 16, 16), 16)
                for i, cols in enumerate(columns(u)):
                    o_params[rows, cols] = par[u, a, b, :, i * 128 : (i + 1) * 128]
        for d in (1, 2, 3):
            reduce_copy(u, d).wait_send()
        for d in (1, 2):
            z_copy(u, d).wait_send()
        for n in (0, 1):
            x_copy(u, n).wait_send()
        w_copy(u).wait_send()

        @pl.when(u < YT)
        def _():
            y_plus(0, 0, u).wait_send()
            y_minus(0, 0, u).wait_send()

    def tick(t, done):
        def stage(f, lag, count=UNITS):
            u = t - lag

            @pl.when((u >= 0) & (u < count))
            def _():
                f(u)

        steps = jnp.where(c == 0, pick(STEPS[0], t), pick(STEPS[1], t))
        lax.fori_loop(done, steps, lambda j, _: pass_on(j), None)
        stage(spread_far, LAG_E)
        stage(spread_x, LAG_D)
        stage(update, LAG_C)
        stage(multiply, 0)
        stage(multiply_hidden, LAG_H)
        stage(finish, LAG_G)
        return steps

    lax.fori_loop(0, UNITS + LAG_G, tick, 0)
    o_hidden[...] = acc[...].astype(BF16)
    for d in (1, 2):
        send(mine, mine, f_s.at[d - 1], f_r.at[d - 1], z_at[d]).wait_send()
        act_copy(d).wait_send()
    for n in range(3):
        bundle(n).wait_send()
    for slot in range(NY):
        across(slot).wait_send()


def write(*refs):
    half = (len(refs) - 1) // 2
    copies = [pltpu.make_async_copy(refs[n], refs[half + n], refs[-1].at[n]) for n in range(half)]
    for copy in copies:
        copy.start()
    for copy in copies:
        copy.wait()


def shards(activations, cotangent, weight, master, moment, second, average):
    rows, width = master.shape
    hidden = weight.shape[0]
    dma = pltpu.SemaphoreType.DMA
    vmem = pltpu.VMEM
    operands = (activations.T, cotangent, weight, master, moment, second, average)
    operands = [pltpu.with_memory_space_constraint(a, pltpu.HBM) for a in operands]
    results = pl.pallas_call(
        kernel,
        out_shape=[vmem((rows, width), F32)] * 4 + [vmem((hidden, width), BF16), vmem((hidden, TOK), BF16)],
        in_specs=[pl.BlockSpec(memory_space=pltpu.HBM)] * 7,
        out_specs=[pl.BlockSpec(memory_space=pltpu.VMEM)] * 6,
        scratch_shapes=[
            vmem((NY, 2, NL, K, FB), BF16),
            vmem((hidden, TOK), BF16),
            vmem((NH, hidden // NH, TOK), BF16),
            vmem((hidden // NH, K), BF16),
            vmem((hidden, width), BF16),
            vmem((4, rows, width), F32),
            vmem((UNITS, 3, 16, UC), BF16),
            vmem((UNITS, 3, 16, UC), BF16),
            vmem((UNITS, 16, UC), F32),
            vmem((UNITS, NX, NH, 16, UC), BF16),
            vmem((hidden, TOK), F32),
            dma((7,)),
            dma((2,)), dma((2,)), dma((2,)), dma((2,)), dma((3,)), dma((3,)),
            dma((YT,)), dma((YT,)), dma((YT,)), dma((YT,)), dma((NY,)), dma((NY,)),
            dma((UNITS, 3)), dma((UNITS, 3)), dma((UNITS, 2)), dma((UNITS, 2)),
            dma((UNITS, 2)), dma((UNITS, 2)), dma((UNITS,)), dma((UNITS,)),
            pltpu.SemaphoreType.REGULAR,
        ],
        compiler_params=pltpu.CompilerParams(
            collective_id=0, has_side_effects=True, vmem_limit_bytes=22 * 1024 * 1024
        ),
    )(*operands)
    shapes = [jax.ShapeDtypeStruct(r.shape, r.dtype) for r in results]
    *updated, hidden_grad = pl.pallas_call(
        write,
        out_shape=shapes,
        in_specs=[pl.BlockSpec(memory_space=pltpu.VMEM)] * 6,
        out_specs=[pl.BlockSpec(memory_space=pl.ANY)] * 6,
        scratch_shapes=[dma((6,))],
        compiler_params=pltpu.CompilerParams(vmem_limit_bytes=1024 * 1024),
    )(*[pltpu.with_memory_space_constraint(r, pltpu.VMEM) for r in results])
    return *updated, hidden_grad.T


def solution(mesh):
    row = P(("shard", "rep"), None)
    both = P("rep", "shard")
    wide = P("shard", None)
    return jax.shard_map(
        shards,
        mesh=mesh,
        in_specs=(both, both, wide, row, row, row, row),
        out_specs=(row, row, row, row, wide, both),
        check_vma=False,
    )
```

time: 95 us -> 87.2 us (0.918)
  the two profiles are of different devices: /device:TPU:24 before, /device:TPU:64 now
where the time goes in v2:
time: 87.2 us; the launch traced here: 87 us
  Pallas kernels  86.4 us (99%)
    pallas_call x1, Pallas kernels, shards(): pl.pallas_call(kernel, out_shape=[vmem((rows, width), F32)] * 4 + [vmem((...  84 us
    pallas_call x1, Pallas kernels, shards(): pl.pallas_call(write, out_shape=shapes, in_specs=[pl.BlockSpec(memory_spa...  2.41 us

profile of v2, /device:TPU:64, one launch (start us, length us, event | category | flops | bytes accessed | tf_op | source)
XLA Modules:
  0.0 87.0 jit_solution(254609256914173194)
XLA Ops:
  0.6 84.0 %shard_map.118 = (f32[16,8192]{1,0:T(8,128)S(1)}, f32[16,8192]{1,0:T(8,128)S(1)}, f32[16,8192]{1,0:T(8,128)S(1)}, f32[16,8192]{1,0:T(8,128)S(1)}, bf16[192,8192]...) custom-call(bf16[192,128]{1,0:T(8,128)(2,1)} %bitcast.2, bf16[128,128]{1,0:T(8,128)(2,1)} %cot.1, bf16[192,8192]{1,0:T(8,128)(2,1)} %weight.1, ...), custom_call_target="tpu_custom_call" | custom-call | tf_op jit(solution)/shard_map/pallas_call | solution.py:327
  84.6 2.4 %shard_map.119 = (f32[16,8192]{1,0:T(8,128)}, f32[16,8192]{1,0:T(8,128)}, f32[16,8192]{1,0:T(8,128)}, f32[16,8192]{1,0:T(8,128)}, bf16[192,8192]{1,0:T(8,128)(2,1)}, /*index=5*/bf16[192,128]{1,0:T(8,128)(2,1)}) custom-call(f32[16,8192]{1,0:T(8,128)S(1)} %get-tuple-element.18.refs_0_, f32[16,8192]{1,0:T(8,128)S(1)} %get-tuple-element.19.refs_1_, ...), custom_call_target="tpu_custom_call" | custom-call | tf_op jit(solution)/shard_map/pallas_call | solution.py:356
